TPU v7x, 32 devices: a whole 2x2x4 slice. The times are simulated.
32 devices in a mesh: grp: 4 (over y, x), dev: 8 (over z, core).
Axes of the slice: x: 2, y: 2, z: 4, core: 2. Of those that a mesh axis runs over, the one named last changes fastest.
Arguments:
- pair_repr: bfloat16 [320, 320, 128], P(('grp', 'dev')), may hold values from -6 to 6
- w_left_gate: bfloat16 [128, 128], replicated, may hold values from -0.5 to 0.5
- w_left: bfloat16 [128, 128], replicated, may hold values from -0.5 to 0.5
- w_right_gate: bfloat16 [128, 128], replicated, may hold values from -0.5 to 0.5
- w_right: bfloat16 [128, 128], replicated, may hold values from -0.5 to 0.5
- w_out_gate: bfloat16 [128, 128], replicated, may hold values from -0.5 to 0.5
- w_out: bfloat16 [128, 128], replicated, may hold values from -0.5 to 0.5
- residue_mask: int32 [320], replicated, may hold values 0 or 1
Outputs:
- update: bfloat16 [320, 320, 128], P(('grp', 'dev'))
Inputs may be any that keep to these rules, and one draw needn't show every extreme that they name: `residue_mask`: 1 marks a residue of the complex, 0 a padded token.
All inputs are finite; a program needn't handle non-finite values.
Results may differ from a plain program's by a relative error of at most 0.0087.
Values may be sent and summed in bfloat16 or wider, within the bound.
A program may use at most 128 MiB of HBM per device.

v0:
```python
import jax
import jax.numpy as jnp
from jax import lax
from jax.sharding import PartitionSpec as P

EPSILON = 1e-05


def layer_norm(values, channel_axis):
    average = jnp.mean(values, axis=channel_axis, keepdims=True)
    centered = values - average
    variance = jnp.mean(centered * centered, axis=channel_axis, keepdims=True)
    return centered * lax.rsqrt(variance + EPSILON)


def gated_proj(normed, weight_gate, weight_value, pair_mask):
    gate_logits = jnp.einsum("rkc,cf->frk", normed, weight_gate, preferred_element_type=jnp.float32)
    projected = jnp.einsum("rkc,cf->frk", normed, weight_value, preferred_element_type=jnp.float32)
    return (jax.nn.sigmoid(gate_logits) * projected * pair_mask[None]).astype(jnp.bfloat16)


def local(pair_repr, w_left_gate, w_left, w_right_gate, w_right, w_out_gate, w_out, residue_mask):
    height = pair_repr.shape[0]
    row_start = (lax.axis_index("grp") * lax.axis_size("dev") + lax.axis_index("dev")) * height
    mask_float = residue_mask.astype(jnp.float32)
    row_mask = lax.dynamic_slice_in_dim(mask_float, row_start, height)
    pair_mask = row_mask[:, None] * mask_float[None, :]
    normed = layer_norm(pair_repr.astype(jnp.float32), 2).astype(jnp.bfloat16)
    left_rows = gated_proj(normed, w_left_gate, w_left, pair_mask)
    right_rows = gated_proj(normed, w_right_gate, w_right, pair_mask)
    out_gate = jax.nn.sigmoid(
        jnp.einsum("rkc,cd->rkd", normed, w_out_gate, preferred_element_type=jnp.float32)
    ).astype(jnp.bfloat16)
    left_cols, right_cols = (
        lax.all_to_all(left_rows, ("grp", "dev"), split_axis=0, concat_axis=1, tiled=True),
        lax.all_to_all(right_rows, ("grp", "dev"), split_axis=0, concat_axis=1, tiled=True),
    )
    product = jnp.einsum(
        "crk,csk->crs", left_cols, right_cols, preferred_element_type=jnp.float32
    ).astype(jnp.bfloat16)
    finish_product = lax.all_to_all(
        product, ("grp", "dev"), split_axis=1, concat_axis=0, tiled=True
    )
    normed_product = layer_norm(finish_product.astype(jnp.float32), 0).astype(jnp.bfloat16)
    mixed_rows = jnp.einsum(
        "crk,cd->rkd", normed_product, w_out, preferred_element_type=jnp.float32
    )
    return (mixed_rows * out_gate).astype(jnp.bfloat16)


def solution(mesh):
    return jax.shard_map(
        local,
        mesh=mesh,
        in_specs=(P(("grp", "dev"), None, None), P(), P(), P(), P(), P(), P(), P()),
        out_specs=P(("grp", "dev"), None, None),
        check_vma=False,
    )
```

profile of v0, /device:TPU:0, one launch (start us, length us, event | category | flops | bytes accessed | tf_op | source)
XLA Modules:
  0.0 138.4 jit_solution(10262706752723988571)
XLA Ops:
  0.0 0.0 copy-start
  0.0 0.0 copy-start.1
  0.0 0.8 convert_element_type.50
  0.8 1.5 %convert_reduce_fusion = f32[10,320]{1,0:T(8,128)S(1)} fusion(bf16[10,320,128]{2,1,0:T(8,128)(2,1)} %param.8), kind=kLoop, calls=%fused_computation.1 | loop fusion | flops 816000 | bytes 832000 | tf_op jit(solution)/shard_map/reduce_sum | solution.py:10
  2.3 0.0 copy-start.5
  2.3 2.2 %fusion.2 = f32[10,320]{1,0:T(8,128)S(1)} fusion(bf16[10,320,128]{2,1,0:T(8,128)(2,1)} %param.8, f32[10,320]{1,0:T(8,128)S(1)} %broadcast_multiply_fusion.2), kind=kLoop, calls=%fused_computation.7 | loop fusion | flops 1635200 | bytes 844800 | tf_op jit(solution)/shard_map/reduce_sum | solution.py:12
  4.5 0.1 dynamic_slice.3
  4.5 0.1 add_rsqrt_fusion.1
  4.6 0.0 copy-done
  4.6 0.0 copy-done.1
  4.6 1.6 %fusion.14 = f32[10,320,128]{2,1,0:T(8,128)S(1)} fusion(bf16[128,128]{1,0:T(8,128)(2,1)S(1)} %copy-done, bf16[10,320,128]{2,1,0:T(8,128)(2,1)S(1)} %copy-done.1, f32[10,320]{1,0:T(8,128)S(1)} %get-tuple-element.5, f32[10,320]{1,0:T(8,128)S(1)} %broadcast_multiply_fusion.2), kind=kOutput, calls=%fused_computation.24 | convolution fusion | flops 106496000 | bytes 2515968 | tf_op jit(solution)/shard_map/rkc,cf->frk/dot_general | solution.py:17
  6.3 0.0 copy-done.5
  6.3 1.7 %fusion.5 = bf16[128,10,320]{0,2,1:T(8,128)(2,1)S(1)} fusion(f32[10,320,128]{2,1,0:T(8,128)S(1)} %fusion.14, f32[10,320]{1,0:T(8,128)S(1)} %get-tuple-element.6, bf16[128,128]{1,0:T(8,128)(2,1)S(1)} %copy-done.5, bf16[10,320,128]{2,1,0:T(8,128)(2,1)S(1)} %copy-done.1, f32[10,320]{1,0:T(8,128)S(1)} %get-tuple-element.5, ...), kind=kOutput, calls=%fused_computation.15 | convolution fusion | flops 108953600 | bytes 3347968 | tf_op jit(solution)/shard_map/rkc,cf->frk/dot_general | solution.py:18
  8.0 2.2 %copy.24 = bf16[128,10,320]{2,1,0:T(8,128)(2,1)} copy(bf16[128,10,320]{0,2,1:T(8,128)(2,1)S(1)} %fusion.5) | data formatting | bytes 1638400 | tf_op jit(solution)/shard_map/convert_element_type | solution.py:19
  10.2 0.0 copy-start.3
  10.2 7.3 %all-to-all-start.1 = ((bf16[128,10,320]{2,1,0:T(8,128)(2,1)}), bf16[128,10,320]{2,1,0:T(8,128)(2,1)S(1)}, u32[]{:S(2)}, u32[]{:S(2)}) async-start(bf16[128,10,320]{2,1,0:T(8,128)(2,1)} %copy.24), calls=%async_computation.1 | async-start | bytes 3145728 | tf_op jit(solution)/shard_map/all_to_all | solution.py:36
  17.5 0.0 copy-done.3
  17.5 0.0 copy-start.6
  17.5 1.7 %fusion.17 = f32[10,320,128]{2,1,0:T(8,128)S(1)} fusion(bf16[128,128]{1,0:T(8,128)(2,1)S(1)} %copy-done.3, bf16[10,320,128]{2,1,0:T(8,128)(2,1)S(1)} %copy-done.1, f32[10,320]{1,0:T(8,128)S(1)} %get-tuple-element.5, f32[10,320]{1,0:T(8,128)S(1)} %broadcast_multiply_fusion.2), kind=kOutput, calls=%fused_computation.27 | convolution fusion | flops 106496000 | bytes 2515968 | tf_op jit(solution)/shard_map/rkc,cf->frk/dot_general | solution.py:17
  19.2 0.0 copy-done.6
  19.2 1.7 %fusion.4 = bf16[128,10,320]{0,2,1:T(8,128)(2,1)S(1)} fusion(f32[10,320,128]{2,1,0:T(8,128)S(1)} %fusion.17, f32[10,320]{1,0:T(8,128)S(1)} %get-tuple-element.6, bf16[128,128]{1,0:T(8,128)(2,1)S(1)} %copy-done.6, bf16[10,320,128]{2,1,0:T(8,128)(2,1)S(1)} %copy-done.1, f32[10,320]{1,0:T(8,128)S(1)} %get-tuple-element.5, ...), kind=kOutput, calls=%fused_computation.14 | convolution fusion | flops 108953600 | bytes 3347968 | tf_op jit(solution)/shard_map/rkc,cf->frk/dot_general | solution.py:18
  20.9 2.1 %copy.21 = bf16[128,10,320]{2,1,0:T(8,128)(2,1)} copy(bf16[128,10,320]{0,2,1:T(8,128)(2,1)S(1)} %fusion.4) | data formatting | bytes 1638400 | tf_op jit(solution)/shard_map/convert_element_type | solution.py:19
  23.0 33.3 %all-to-all-done.1 = bf16[128,10,320]{2,1,0:T(8,128)(2,1)S(1)} async-done(((bf16[128,10,320]{2,1,0:T(8,128)(2,1)}), bf16[128,10,320]{2,1,0:T(8,128)(2,1)S(1)}, u32[]{:S(2)}, u32[]{:S(2)}) %all-to-all-start.1) | async-done | bytes 819232 | tf_op jit(solution)/shard_map/all_to_all | solution.py:36
  56.4 3.4 %all-to-all-start = ((bf16[128,10,320]{2,1,0:T(8,128)(2,1)}), bf16[128,10,320]{2,1,0:T(8,128)(2,1)}, u32[]{:S(2)}, u32[]{:S(2)}) async-start(bf16[128,10,320]{2,1,0:T(8,128)(2,1)} %copy.21), calls=%async_computation | async-start | bytes 3145728 | tf_op jit(solution)/shard_map/all_to_all | solution.py:35
  59.8 0.4 copy.36
  60.2 38.5 %all-to-all-done = bf16[128,10,320]{2,1,0:T(8,128)(2,1)} async-done(((bf16[128,10,320]{2,1,0:T(8,128)(2,1)}), bf16[128,10,320]{2,1,0:T(8,128)(2,1)}, u32[]{:S(2)}, u32[]{:S(2)}) %all-to-all-start) | async-done | bytes 819232 | tf_op jit(solution)/shard_map/all_to_all | solution.py:35
  98.7 1.8 %copy.34 = bf16[32,4,10,320]{3,1,2,0:T(4,128)(2,1)S(1)} copy(bf16[32,4,10,320]{3,2,1,0:T(8,128)(2,1)} %bitcast.3) | data formatting | bytes 1638400 | tf_op jit(solution)/shard_map/all_to_all | solution.py:35
  100.4 0.8 convolution_convert_fusion
  101.2 0.0 copy-start.7
  101.3 1.7 %copy.29 = bf16[4,320,320]{2,0,1:T(4,128)(2,1)} copy(bf16[4,320,320]{2,1,0:T(8,128)(2,1)S(1)} %convolution_convert_fusion) | data formatting | bytes 1638400 | tf_op jit(solution)/shard_map/convert_element_type | solution.py:40
  103.0 2.6 %all-to-all-start.2 = ((bf16[4,320,320]{2,0,1:T(4,128)(2,1)}), bf16[4,320,320]{2,0,1:T(4,128)(2,1)S(1)}, u32[]{:S(2)}, u32[]{:S(2)}) async-start(bf16[4,320,320]{2,0,1:T(4,128)(2,1)} %copy.29), calls=%async_computation.2 | async-start | bytes 1966080 | tf_op jit(solution)/shard_map/all_to_all | solution.py:41
  105.6 0.0 copy-done.7
  105.6 2.1 %divide_convert_fusion = bf16[10,320,128]{2,1,0:T(8,128)(2,1)} fusion(bf16[128,128]{1,0:T(8,128)(2,1)S(1)} %copy-done.7, bf16[10,320,128]{2,1,0:T(8,128)(2,1)S(1)} %copy-done.1, f32[10,320]{1,0:T(8,128)S(1)} %get-tuple-element.5, f32[10,320]{1,0:T(8,128)S(1)} %broadcast_multiply_fusion.2), kind=kOutput, calls=%fused_computation.12 | convolution fusion | flops 108134400 | bytes 1696768 | tf_op jit(solution)/shard_map/rkc,cd->rkd/dot_general | solution.py:32
  107.7 24.1 %all-to-all-done.2 = bf16[4,320,320]{2,0,1:T(4,128)(2,1)S(1)} async-done(((bf16[4,320,320]{2,0,1:T(4,128)(2,1)}), bf16[4,320,320]{2,0,1:T(4,128)(2,1)S(1)}, u32[]{:S(2)}, u32[]{:S(2)}) %all-to-all-start.2) | async-done | bytes 819232 | tf_op jit(solution)/shard_map/all_to_all | solution.py:41
  131.8 0.5 fusion.6
  132.3 0.3 convert_bitcast_fusion
  132.5 0.7 multiply_reduce_fusion
  133.3 1.7 %copy.30 = f32[32,4,10,320]{3,1,0,2:T(4,128)} copy(f32[32,4,10,320]{3,1,2,0:T(4,128)S(1)} %convert_bitcast_fusion) | data formatting | bytes 3276800 | tf_op jit(solution)/shard_map/convert_element_type | solution.py:44
  135.0 0.0 copy-start.2
  135.0 0.0 copy-start.4
  135.0 2.0 %reshape.57 = f32[128,10,320]{2,0,1:T(8,128)S(1)} reshape(f32[32,4,10,320]{3,1,0,2:T(4,128)} %copy.30) | data formatting | bytes 3276800 | tf_op jit(solution)/shard_map/convert_element_type | solution.py:44
  137.0 0.0 copy-done.2
  137.0 0.0 copy-done.4
  137.1 1.4 multiply_convert_fusion.3
  (3 shorter events, 0.0 us)
Async XLA Ops:
  0.0 4.6 %copy-start = (bf16[128,128]{1,0:T(8,128)(2,1)S(1)}, bf16[128,128]{1,0:T(8,128)(2,1)}, u32[]{:S(2)}) copy-start(bf16[128,128]{1,0:T(8,128)(2,1)} %param.11) | copy-start | bytes 98308
  0.0 4.6 %copy-start.1 = (bf16[10,320,128]{2,1,0:T(8,128)(2,1)S(1)}, bf16[10,320,128]{2,1,0:T(8,128)(2,1)}, u32[]{:S(2)}) copy-start(bf16[10,320,128]{2,1,0:T(8,128)(2,1)} %param.8) | copy-start | bytes 2457604
  2.3 4.0 %copy-start.5 = (bf16[128,128]{1,0:T(8,128)(2,1)S(1)}, bf16[128,128]{1,0:T(8,128)(2,1)}, u32[]{:S(2)}) copy-start(bf16[128,128]{1,0:T(8,128)(2,1)} %param.12) | copy-start | bytes 98308
  10.2 7.3 %copy-start.3 = (bf16[128,128]{1,0:T(8,128)(2,1)S(1)}, bf16[128,128]{1,0:T(8,128)(2,1)}, u32[]{:S(2)}) copy-start(bf16[128,128]{1,0:T(8,128)(2,1)} %param.9) | copy-start | bytes 98308
  10.2 46.2 %all-to-all-start.1 = ((bf16[128,10,320]{2,1,0:T(8,128)(2,1)}), bf16[128,10,320]{2,1,0:T(8,128)(2,1)S(1)}, u32[]{:S(2)}, u32[]{:S(2)}) async-start(bf16[128,10,320]{2,1,0:T(8,128)(2,1)} %copy.24), calls=%async_computation.1 | async-start | bytes 3145728 | tf_op jit(solution)/shard_map/all_to_all | solution.py:36
  17.5 1.7 %copy-start.6 = (bf16[128,128]{1,0:T(8,128)(2,1)S(1)}, bf16[128,128]{1,0:T(8,128)(2,1)}, u32[]{:S(2)}) copy-start(bf16[128,128]{1,0:T(8,128)(2,1)} %param.10) | copy-start | bytes 98308
  56.4 42.3 %all-to-all-start = ((bf16[128,10,320]{2,1,0:T(8,128)(2,1)}), bf16[128,10,320]{2,1,0:T(8,128)(2,1)}, u32[]{:S(2)}, u32[]{:S(2)}) async-start(bf16[128,10,320]{2,1,0:T(8,128)(2,1)} %copy.21), calls=%async_computation | async-start | bytes 3145728 | tf_op jit(solution)/shard_map/all_to_all | solution.py:35
  101.2 4.4 %copy-start.7 = (bf16[128,128]{1,0:T(8,128)(2,1)S(1)}, bf16[128,128]{1,0:T(8,128)(2,1)}, u32[]{:S(2)}) copy-start(bf16[128,128]{1,0:T(8,128)(2,1)} %param.13) | copy-start | bytes 98308
  103.0 28.8 %all-to-all-start.2 = ((bf16[4,320,320]{2,0,1:T(4,128)(2,1)}), bf16[4,320,320]{2,0,1:T(4,128)(2,1)S(1)}, u32[]{:S(2)}, u32[]{:S(2)}) async-start(bf16[4,320,320]{2,0,1:T(4,128)(2,1)} %copy.29), calls=%async_computation.2 | async-start | bytes 1966080 | tf_op jit(solution)/shard_map/all_to_all | solution.py:41
  135.0 2.0 %copy-start.2 = (bf16[10,320,128]{2,1,0:T(8,128)(2,1)S(1)}, bf16[10,320,128]{2,1,0:T(8,128)(2,1)}, u32[]{:S(2)}) copy-start(bf16[10,320,128]{2,1,0:T(8,128)(2,1)} %divide_convert_fusion) | copy-start | bytes 2457604
  135.0 2.1 %copy-start.4 = (bf16[128,128]{1,0:T(8,128)(2,1)S(1)}, bf16[128,128]{1,0:T(8,128)(2,1)}, u32[]{:S(2)}) copy-start(bf16[128,128]{1,0:T(8,128)(2,1)} %param.14) | copy-start | bytes 98308
where the time goes:
time: 139 us; the launch traced here: 138 us
  waiting for transfers between devices  95.9 us (69%)
  starting transfers between devices  13.4 us (10%)
  local copies, waits for them, and re-layouts  12 us (9%)
  matrix products  11 us (8%)
  other arithmetic  5.93 us (4%)
    all_to_all x1, waiting for transfers between devices, local(): lax.all_to_all(left_rows, ('grp', 'dev'), split_axis=0, concat_axis=1, ti...  38.5 us
    all_to_all x1, waiting for transfers between devices, local(): lax.all_to_all(right_rows, ('grp', 'dev'), split_axis=0, concat_axis=1, t...  33.3 us
    all_to_all x1, waiting for transfers between devices, local(): lax.all_to_all(product, ('grp', 'dev'), split_axis=1, concat_axis=0, tile...  24.1 us
    all_to_all x1, starting transfers between devices, local(): lax.all_to_all(right_rows, ('grp', 'dev'), split_axis=0, concat_axis=1, t...  7.3 us
    convert_element_type x2, local copies, waits for them, and re-layouts, gated_proj(): (jax.nn.sigmoid(gate_logits) * projected * pair_mask[None]).astype(jnp.bf...  4.28 us
    convert_element_type x2, local copies, waits for them, and re-layouts, local(): finish_product.astype(jnp.float32)  3.75 us
    dot_general x2, matrix products, gated_proj(): jnp.einsum('rkc,cf->frk', normed, weight_value, preferred_element_type=jn...  3.45 us
    all_to_all x1, starting transfers between devices, local(): lax.all_to_all(left_rows, ('grp', 'dev'), split_axis=0, concat_axis=1, ti...  3.42 us
  transfers between devices with their start and end apart: 3, of which 3 were waited for; matrix products, arithmetic and copies ran while one was open for 6% of the time, Pallas kernels for 0%

commit v1 on v0

--- a/solution.py
+++ b/solution.py
@@ -1,6 +1,10 @@
+import functools
+
 import jax
 import jax.numpy as jnp
 from jax import lax
+from jax.experimental import pallas as pl
+from jax.experimental.pallas import tpu as pltpu
 from jax.sharding import PartitionSpec as P
 
 EPSILON = 1e-05
@@ -48,9 +52,398 @@
     return (mixed_rows * out_gate).astype(jnp.bfloat16)
 
 
+MESH = pl.DeviceIdType.MESH
+
+
+def sigmoid(x):
+    return 1.0 / (1.0 + jnp.exp(-x))
+
+
+def fused_kernel(
+    n_grp, n_dev,
+    x_ref, wlg_ref, wl_ref, wrg_ref, wr_ref, wog_ref, wo_ref, mask_ref, mask_s,
+    out_ref,
+    nbuf, r_src, l_src, p_src, r_buf, l_buf, p_buf, stage, l_mat, r_mat, y_buf,
+    ra_send, l_send, p_send, z_send, r_recv, l_recv, p_recv, loc_sem,
+):
+    rows, tokens, chans = x_ref.shape
+    half = rows // 2
+    n_plane, _, ch, width = r_src.shape
+    nz = n_dev // 2
+    main = tokens // 128 * 128
+    tail = tokens - main
+    tiles = main // 128
+    plane_rows = n_plane * rows
+    grp = lax.axis_index("grp")
+    dev = lax.axis_index("dev")
+    z = dev // 2
+    core = lax.rem(dev, 2)
+    q = grp * 2 + core
+
+    def plane_peer(other):
+        return (other // 2, z * 2 + lax.rem(other, 2))
+
+    def other_of(o):
+        return lax.rem(q + o, n_plane)
+
+    barrier = pltpu.get_barrier_semaphore()
+
+    @pl.loop(1, n_plane)
+    def _(o):
+        pl.semaphore_signal(barrier, inc=1, device_id=plane_peer(other_of(o)), device_id_type=MESH)
+
+    @pl.when(z > 0)
+    def _():
+        pl.semaphore_signal(barrier, inc=1, device_id=(grp, dev - 2), device_id_type=MESH)
+
+    @pl.when(z < nz - 1)
+    def _():
+        pl.semaphore_signal(barrier, inc=1, device_id=(grp, dev + 2), device_id_type=MESH)
+
+    mask = mask_ref[...].astype(jnp.float32)
+    pieces = [mask[:, :main], mask[:, :main]]
+    if tail:
+        pieces += [mask[:, main:], mask[:, main:]]
+    mask2 = jnp.concatenate(pieces, axis=1)
+    lane = lax.broadcasted_iota(jnp.int32, (1, width), 1)
+    first = (lane < main) | ((lane >= 2 * main) & (lane < 2 * main + tail))
+    row0 = (grp * n_dev + dev) * rows
+
+    def norm_rows(v):
+        v = v.astype(jnp.float32)
+        c = v - jnp.mean(v, axis=-1, keepdims=True)
+        var = jnp.mean(c * c, axis=-1, keepdims=True)
+        return (c * lax.rsqrt(var + EPSILON)).astype(jnp.bfloat16)
+
+    def project(n, p, wg_t, wv_t, dst):
+        nt = (((1,), (1,)), ((), ()))
+        gate = lax.dot_general(wg_t, n, nt, preferred_element_type=jnp.float32)
+        value = lax.dot_general(wv_t, n, nt, preferred_element_type=jnp.float32)
+        m0 = mask_s[row0 + p].astype(jnp.float32)
+        m1 = mask_s[row0 + half + p].astype(jnp.float32)
+        m = mask2 * jnp.where(first, m0, m1)
+        res = (sigmoid(gate) * value * m).astype(jnp.bfloat16)
+        for k in range(n_plane):
+            dst[k, p] = res[k * ch:(k + 1) * ch]
+
+    wrg_t, wr_t = wrg_ref[...].T, wr_ref[...].T
+
+    @pl.loop(0, half)
+    def _(p):
+        a, b = norm_rows(x_ref[p]), norm_rows(x_ref[p + half])
+        parts = [a[:main], b[:main]]
+        if tail:
+            parts += [a[main:], b[main:]]
+        n = jnp.concatenate(parts, axis=0)
+        nbuf[p] = n
+        project(n, p, wrg_t, wr_t, r_src)
+
+    pl.semaphore_wait(
+        barrier,
+        n_plane - 1 + jnp.where(z > 0, 1, 0) + jnp.where(z < nz - 1, 1, 0),
+    )
+
+    def plane_copy(src, dst, send, recv, to):
+        return pltpu.make_async_remote_copy(
+            src_ref=src, dst_ref=dst, send_sem=send, recv_sem=recv,
+            device_id=plane_peer(to), device_id_type=MESH)
+
+    def z_copy(src, zz, s, up):
+        return pltpu.make_async_remote_copy(
+            src_ref=src, dst_ref=r_buf.at[zz, s], send_sem=z_send.at[1 if up else 0, zz, s],
+            recv_sem=r_recv.at[zz, s], device_id=(grp, dev + (2 if up else -2)), device_id_type=MESH)
+
+    def ra_copy(o):
+        t = other_of(o)
+        return plane_copy(r_src.at[t], r_buf.at[z, q], ra_send.at[o], r_recv.at[z, q], t)
+
+    def l_copy(o):
+        t = other_of(o)
+        return plane_copy(l_src.at[t], l_buf.at[q], l_send.at[o], l_recv.at[q], t)
+
+    def p_copy(t):
+        return plane_copy(p_src.at[t], p_buf.at[q], p_send.at[t], p_recv.at[q], t)
+
+    def wait_plane(dst, recv, s):
+        plane_copy(dst, dst, recv, recv, s).wait_recv()
+
+    @pl.when(z < nz - 1)
+    def _():
+        z_copy(r_src.at[q], z, q, True).start()
+
+    @pl.when(z > 0)
+    def _():
+        z_copy(r_src.at[q], z, q, False).start()
+
+    @pl.loop(1, n_plane)
+    def _(o):
+        ra_copy(o).start()
+
+    own_r = pltpu.make_async_copy(r_src.at[q], r_buf.at[z, q], loc_sem.at[0])
+    own_r.start()
+
+    wlg_t, wl_t = wlg_ref[...].T, wl_ref[...].T
+
+    @pl.loop(0, half)
+    def _(p):
+        project(nbuf[p], p, wlg_t, wl_t, l_src)
+
+    @pl.loop(1, n_plane)
+    def _(o):
+        l_copy(o).start()
+
+    own_l = pltpu.make_async_copy(l_src.at[q], l_buf.at[q], loc_sem.at[1])
+    own_l.start()
+
+    @pl.loop(1, n_plane)
+    def _(o):
+        s = other_of(o)
+        wait_plane(r_buf.at[z, s], r_recv.at[z, s], s)
+
+        @pl.when(z < nz - 1)
+        def _():
+            z_copy(r_buf.at[z, s], z, s, True).start()
+
+        @pl.when(z > 0)
+        def _():
+            z_copy(r_buf.at[z, s], z, s, False).start()
+
+    wog = wog_ref[...]
+
+    @pl.loop(0, half)
+    def _(p):
+        g = sigmoid(jnp.dot(nbuf[p], wog, preferred_element_type=jnp.float32)).astype(jnp.bfloat16)
+        out_ref[p, :main] = g[:main]
+        out_ref[p + half, :main] = g[main:2 * main]
+        if tail:
+            out_ref[p, main:] = g[2 * main:2 * main + tail]
+            out_ref[p + half, main:] = g[2 * main + tail:]
+
+    lane1 = lax.broadcasted_iota(jnp.int32, (1, 128), 1)
+
+    def unpack(block, s, masked):
+        for p in range(half):
+            v = block[p].astype(jnp.float32)
+            for b in range(2):
+                where = pl.ds(s * rows + p + b * half, ch, stride=plane_rows)
+                for t in range(tiles):
+                    stage[t, where, :] = v[:, b * main + t * 128:b * main + (t + 1) * 128]
+                if tail:
+                    u = v[:, 2 * main:]
+                    if b:
+                        u = pltpu.roll(u, tail, 1)
+                    if masked:
+                        u = jnp.where(lane1 < tail, u, 0.0)
+                    stage[tiles, where, :] = u
+
+    n_tiles = tiles + (1 if tail else 0)
+
+    def settle(dst):
+        for c in range(ch):
+            for t in range(n_tiles):
+                dst(c, t, stage[t, c * plane_rows:(c + 1) * plane_rows, :].astype(jnp.bfloat16))
+
+    own_l.wait()
+
+    @pl.loop(1, n_plane)
+    def _(o):
+        s = other_of(o)
+        wait_plane(l_buf.at[s], l_recv.at[s], s)
+
+    @pl.loop(0, n_plane)
+    def _(s):
+        unpack(l_buf.at[s], s, True)
+
+    def to_left(c, t, v):
+        l_mat[c, :, t * 128:(t + 1) * 128] = v
+
+    settle(to_left)
+
+    def take_plane(zz):
+        @pl.loop(0, n_plane)
+        def _(s):
+            unpack(r_buf.at[zz, s], s, False)
+
+        def to_right(c, t, v):
+            r_mat[c, zz, :, t * 128:(t + 1) * 128] = v
+
+        settle(to_right)
+
+    own_r.wait()
+    take_plane(z)
+
+    @pl.loop(1, nz)
+    def _(h):
+        lo, hi = z - h, z + h
+
+        @pl.loop(0, n_plane)
+        def _(o):
+            s = other_of(o)
+
+            @pl.when(lo >= 0)
+            def _():
+                z_copy(r_buf.at[lo, s], lo, s, True).wait_recv()
+
+                @pl.when(z < nz - 1)
+                def _():
+                    z_copy(r_buf.at[lo, s], lo, s, True).start()
+
+            @pl.when(hi <= nz - 1)
+            def _():
+                z_copy(r_buf.at[hi, s], hi, s, False).wait_recv()
+
+                @pl.when(z > 0)
+                def _():
+                    z_copy(r_buf.at[hi, s], hi, s, False).start()
+
+        @pl.when(lo >= 0)
+        def _():
+            take_plane(lo)
+
+        @pl.when(hi <= nz - 1)
+        def _():
+            take_plane(hi)
+
+    for c in range(ch):
+        prod = lax.dot_general(
+            l_mat[c], r_mat[c].reshape(nz * plane_rows, n_tiles * 128), (((1,), (1,)), ((), ())),
+            preferred_element_type=jnp.float32)
+        for t in range(tiles):
+            stage[t, c * plane_rows:(c + 1) * plane_rows, :] = prod[:, t * 128:(t + 1) * 128]
+        if tail:
+            stage[tiles, c * plane_rows:(c + 1) * plane_rows, :tail] = prod[:, main:]
+
+    @pl.loop(1, n_plane + 1)
+    def _(o):
+        to = other_of(o)
+        for p in range(half):
+            pair = []
+            ends = []
+            for b in range(2):
+                where = pl.ds(to * rows + p + b * half, ch, stride=plane_rows)
+                pair += [stage[t, where, :] for t in range(tiles)]
+                if tail:
+                    ends.append(stage[tiles, where, :])
+            if tail:
+                pair.append(jnp.where(lane1 < tail, ends[0], pltpu.roll(ends[1], tail, 1)))
+            p_src[to, p] = jnp.concatenate(pair, axis=1).astype(jnp.bfloat16)
+
+        @pl.when(o < n_plane)
+        def _():
+            p_copy(to).start()
+
+    own_p = pltpu.make_async_copy(p_src.at[q], p_buf.at[q], loc_sem.at[2])
+    own_p.start()
+    own_p.wait()
+
+    @pl.loop(1, n_plane)
+    def _(o):
+        s = other_of(o)
+        wait_plane(p_buf.at[s], p_recv.at[s], s)
+
+    wo = wo_ref[...]
+    piece = 2 * rows
+
+    @pl.loop(0, half)
+    def _(p):
+        v = jnp.concatenate([p_buf[k, p] for k in range(n_plane)], axis=0).astype(jnp.float32)
+        c = v - jnp.mean(v, axis=0, keepdims=True)
+        var = jnp.mean(c * c, axis=0, keepdims=True)
+        n = (c * lax.rsqrt(var + EPSILON)).astype(jnp.bfloat16)
+        y = lax.dot_general(n, wo, (((0,), (0,)), ((), ())), preferred_element_type=jnp.float32)
+        for b in range(2):
+            parts = [y[b * main:(b + 1) * main]]
+            if tail:
+                parts.append(y[2 * main + b * tail:2 * main + (b + 1) * tail])
+            full = jnp.concatenate(parts, axis=0)
+            for zz in range(nz):
+                for gg in range(n_grp):
+                    y_buf[b, (gg * nz + zz) * piece:(gg * nz + zz + 1) * piece, :] = (
+                        full[(zz * n_grp + gg) * piece:(zz * n_grp + gg + 1) * piece])
+            row = p + b * half
+            out_ref[row] = (y_buf[b] * out_ref[row].astype(jnp.float32)).astype(jnp.bfloat16)
+
+    @pl.loop(1, n_plane)
+    def _(o):
+        ra_copy(o).wait_send()
+        l_copy(o).wait_send()
+        p_copy(other_of(o)).wait_send()
+
+    @pl.loop(0, nz)
+    def _(zz):
+        @pl.loop(0, n_plane)
+        def _(s):
+            @pl.when((zz <= z) & (z < nz - 1))
+            def _():
+                z_copy(r_buf.at[zz, s], zz, s, True).wait_send()
+
+            @pl.when((zz >= z) & (z > 0))
+            def _():
+                z_copy(r_buf.at[zz, s], zz, s, False).wait_send()
+
+
+def fused(mesh, args):
+    n_grp, n_dev = mesh.shape["grp"], mesh.shape["dev"]
+    x, residue_mask = args[0], args[-1]
+    rows, tokens, chans = x.shape
+    n_plane, nz, half = n_grp * 2, n_dev // 2, rows // 2
+    ch = args[1].shape[1] // n_plane
+    width = 2 * tokens
+    n_tiles = -(-tokens // 128)
+    bf, f32 = jnp.bfloat16, jnp.float32
+    blocks = (n_plane, half, ch, width)
+    vmem = pl.BlockSpec(memory_space=pltpu.VMEM)
+    dma = pltpu.SemaphoreType.DMA
+    return pl.pallas_call(
+        functools.partial(fused_kernel, n_grp, n_dev),
+        out_shape=jax.ShapeDtypeStruct(x.shape, bf),
+        in_specs=[vmem] * 8 + [pl.BlockSpec(memory_space=pltpu.SMEM)],
+        out_specs=vmem,
+        scratch_shapes=[
+            pltpu.VMEM((half, width, chans), bf),
+            pltpu.VMEM(blocks, bf),
+            pltpu.VMEM(blocks, bf),
+            pltpu.VMEM(blocks, bf),
+            pltpu.VMEM((nz,) + blocks, bf),
+            pltpu.VMEM(blocks, bf),
+            pltpu.VMEM(blocks, bf),
+            pltpu.VMEM((n_tiles, ch * n_plane * rows, 128), f32),
+            pltpu.VMEM((ch, n_plane * rows, n_tiles * 128), bf),
+            pltpu.VMEM((ch, nz, n_plane * rows, n_tiles * 128), bf),
+            pltpu.VMEM((2, tokens, chans), f32),
+            dma((n_plane,)),
+            dma((n_plane,)),
+            dma((n_plane,)),
+            dma((2, nz, n_plane)),
+            dma((nz, n_plane)),
+            dma((n_plane,)),
+            dma((n_plane,)),
+            dma((3,)),
+        ],
+        compiler_params=pltpu.CompilerParams(
+            collective_id=0, has_side_effects=True, vmem_limit_bytes=48 * 1024 * 1024),
+        cost_estimate=pl.CostEstimate(flops=10**9, bytes_accessed=10**7, transcendentals=10**6),
+    )(*args[:-1], residue_mask.reshape(1, tokens), residue_mask)
+
+
+def fits(mesh, tokens, hidden):
+    n_plane, nz = mesh.shape["grp"] * 2, mesh.shape["dev"] // 2
+    rows = tokens // (n_plane * nz)
+    if mesh.shape["dev"] % 2 or hidden % n_plane or (hidden // n_plane) % 16:
+        return False
+    if rows % 2 or (n_plane * rows) % 16 or tokens % 128 not in (0, 64):
+        return False
+    return 4 * (hidden // n_plane) * tokens * tokens < 16 * 1024 * 1024
+
+
 def solution(mesh):
+    def body(*args):
+        if fits(mesh, args[-1].shape[0], args[1].shape[1]):
+            return fused(mesh, args)
+        return local(*args)
+
     return jax.shard_map(
-        local,
+        body,
         mesh=mesh,
         in_specs=(P(("grp", "dev"), None, None), P(), P(), P(), P(), P(), P(), P()),
         out_specs=P(("grp", "dev"), None, None),

time: 139 us -> 89.6 us (0.64)
  waiting for transfers between devices: 95.9 us -> 0 us
  Pallas kernels: 0 us -> 81.2 us
  starting transfers between devices: 13.4 us -> 0 us
  matrix products: 11 us -> 0 us
  other arithmetic: 5.93 us -> 0 us
  local copies, waits for them, and re-layouts: 12 us -> 7.34 us
    all_to_all x3 -> x0, waiting for transfers between devices: 95.9 us -> none  [the longest x1 38.5 us: local(): lax.all_to_all(left_rows, ('grp', 'dev'), split_axis=0, concat_axis=1, ti...]
    pallas_call x0 -> x1, Pallas kernels: none -> 81.2 us  [fused(): pl.pallas_call(functools.partial(fused_kernel, n_grp, n_dev), out_shape=j...]
    all_to_all x3 -> x0, starting transfers between devices: 13.4 us -> none  [the longest x1 7.3 us: local(): lax.all_to_all(right_rows, ('grp', 'dev'), split_axis=0, concat_axis=1, t...]
    dot_general x7 -> x0, matrix products: 11 us -> none  [the longest x2 3.45 us: gated_proj(): jnp.einsum('rkc,cf->frk', normed, weight_value, preferred_element_type=jn...]
    convert_element_type x5 -> x0, local copies, waits for them, and re-layouts: 9.76 us -> none  [the longest x2 4.28 us: gated_proj(): (jax.nn.sigmoid(gate_logits) * projected * pair_mask[None]).astype(jnp.bf...]
    unnamed x16 -> x17, local copies, waits for them, and re-layouts: 0.04 us -> 6.59 us
    reduce_sum x4 -> x0, other arithmetic: 4.82 us -> none  [the longest x2 2.88 us: layer_norm(): variance = jnp.mean(centered * centered, axis=channel_axis, keepdims=True)]
    all_to_all x2 -> x0, local copies, waits for them, and re-layouts: 2.17 us -> none  [the longest x1 1.79 us: local(): lax.all_to_all(left_rows, ('grp', 'dev'), split_axis=0, concat_axis=1, ti...]
  transfers between devices with their start and end apart: 3 -> 0, of which waited for: 3 -> 0; matrix products, arithmetic and copies ran while one was open for 6% -> 0% of each run, Pallas kernels for 0% -> 0%
where the time goes in v1:
time: 89.6 us; the launch traced here: 88.6 us
  Pallas kernels  81.2 us (91%)
  local copies, waits for them, and re-layouts  7.34 us (8%)
    pallas_call x1, Pallas kernels, fused(): pl.pallas_call(functools.partial(fused_kernel, n_grp, n_dev), out_shape=j...  81.2 us
    unnamed x17, local copies, waits for them, and re-layouts  6.59 us

profile of v1, /device:TPU:0, one launch (start us, length us, event | category | flops | bytes accessed | tf_op | source)
XLA Modules:
  0.0 88.6 jit_solution(4994687331836313908)
XLA Ops:
  0.0 0.0 copy-start
  0.0 0.8 reshape.3.mask_ref
  0.8 0.0 copy-done
  0.8 0.0 copy-start.1
  0.8 1.1 %copy-done.1 = bf16[10,320,128]{2,1,0:T(8,128)(2,1)S(1)} copy-done((bf16[10,320,128]{2,1,0:T(8,128)(2,1)S(1)}, bf16[10,320,128]{2,1,0:T(8,128)(2,1)}, u32[]{:S(2)}) %copy-start.1) | copy-done | bytes 819224
  1.9 0.0 copy-start.2
  1.9 0.8 copy-done.2
  2.7 0.0 copy-start.3
  2.7 0.8 copy-done.3
  3.4 0.0 copy-start.4
  3.4 0.8 copy-done.4
  4.2 0.0 copy-start.5
  4.2 0.8 copy-done.5
  4.9 0.0 copy-start.6
  4.9 0.8 copy-done.6
  5.7 0.0 copy-start.7
  5.7 0.8 copy-done.7
  6.5 81.2 %shard_map.82 = bf16[10,320,128]{2,1,0:T(8,128)(2,1)S(1)} custom-call(bf16[10,320,128]{2,1,0:T(8,128)(2,1)S(1)} %copy-done.1, bf16[128,128]{1,0:T(8,128)(2,1)S(1)} %copy-done.2, bf16[128,128]{1,0:T(8,128)(2,1)S(1)} %copy-done.3, bf16[128,128]{1,0:T(8,128)(2,1)S(1)} %copy-done.4, bf16[128,128]{1,0:T(8,128)(2,1)S(1)} %copy-done.5, ...), custom_call_target="tpu_custom_call" | custom-call | flops 1000000000 | bytes 10000000 | tf_op jit(solution)/shard_map/pallas_call | solution.py:397
  87.7 0.9 %copy.10 = bf16[10,320,128]{2,1,0:T(8,128)(2,1)} copy(bf16[10,320,128]{2,1,0:T(8,128)(2,1)S(1)} %shard_map.82) | data formatting | bytes 1638400
Async XLA Ops:
  0.0 0.8 copy-start
  0.8 1.1 %copy-start.1 = (bf16[10,320,128]{2,1,0:T(8,128)(2,1)S(1)}, bf16[10,320,128]{2,1,0:T(8,128)(2,1)}, u32[]{:S(2)}) copy-start(bf16[10,320,128]{2,1,0:T(8,128)(2,1)} %x_ref.1) | copy-start | bytes 2457604
  1.9 0.8 copy-start.2
  2.7 0.8 copy-start.3
  3.4 0.8 copy-start.4
  4.2 0.8 copy-start.5
  4.9 0.8 copy-start.6
  5.7 0.8 copy-start.7

commit v2 on v1

v2 whole, which is shorter than its diff:
```python
import functools

import jax
import jax.numpy as jnp
from jax import lax
from jax.experimental import pallas as pl
from jax.experimental.pallas import tpu as pltpu
from jax.sharding import PartitionSpec as P

EPSILON = 1e-05


def layer_norm(values, channel_axis):
    average = jnp.mean(values, axis=channel_axis, keepdims=True)
    centered = values - average
    variance = jnp.mean(centered * centered, axis=channel_axis, keepdims=True)
    return centered * lax.rsqrt(variance + EPSILON)


def gated_proj(normed, weight_gate, weight_value, pair_mask):
    gate_logits = jnp.einsum("rkc,cf->frk", normed, weight_gate, preferred_element_type=jnp.float32)
    projected = jnp.einsum("rkc,cf->frk", normed, weight_value, preferred_element_type=jnp.float32)
    return (jax.nn.sigmoid(gate_logits) * projected * pair_mask[None]).astype(jnp.bfloat16)


def local(pair_repr, w_left_gate, w_left, w_right_gate, w_right, w_out_gate, w_out, residue_mask):
    height = pair_repr.shape[0]
    row_start = (lax.axis_index("grp") * lax.axis_size("dev") + lax.axis_index("dev")) * height
    mask_float = residue_mask.astype(jnp.float32)
    row_mask = lax.dynamic_slice_in_dim(mask_float, row_start, height)
    pair_mask = row_mask[:, None] * mask_float[None, :]
    normed = layer_norm(pair_repr.astype(jnp.float32), 2).astype(jnp.bfloat16)
    left_rows = gated_proj(normed, w_left_gate, w_left, pair_mask)
    right_rows = gated_proj(normed, w_right_gate, w_right, pair_mask)
    out_gate = jax.nn.sigmoid(
        jnp.einsum("rkc,cd->rkd", normed, w_out_gate, preferred_element_type=jnp.float32)
    ).astype(jnp.bfloat16)
    left_cols, right_cols = (
        lax.all_to_all(left_rows, ("grp", "dev"), split_axis=0, concat_axis=1, tiled=True),
        lax.all_to_all(right_rows, ("grp", "dev"), split_axis=0, concat_axis=1, tiled=True),
    )
    product = jnp.einsum(
        "crk,csk->crs", left_cols, right_cols, preferred_element_type=jnp.float32
    ).astype(jnp.bfloat16)
    finish_product = lax.all_to_all(
        product, ("grp", "dev"), split_axis=1, concat_axis=0, tiled=True
    )
    normed_product = layer_norm(finish_product.astype(jnp.float32), 0).astype(jnp.bfloat16)
    mixed_rows = jnp.einsum(
        "crk,cd->rkd", normed_product, w_out, preferred_element_type=jnp.float32
    )
    return (mixed_rows * out_gate).astype(jnp.bfloat16)


MESH = pl.DeviceIdType.MESH
HALVES = 2
PLANES = 4


def sigmoid(x):
    return 1.0 / (1.0 + jnp.exp(-x))


def fused_kernel(
    n_grp, n_dev,
    x_hbm, wlg_hbm, wl_hbm, wrg_hbm, wr_hbm, wog_hbm, wo_hbm, mask_hbm,
    out_ref,
    x_ref, wlg_ref, wl_ref, wrg_ref, wr_ref, wog_ref, wo_ref, mask_ref, mask_s,
    nbuf, r_src, l_src, p_src, r_buf, l_buf, p_buf, stage, l_mat, r_mat, y_buf,
    ra_send, l_send, p_send, z_send, lz_send, r_recv, l_recv, p_recv, loc_sem, in_sem,
):
    rows, tokens, chans = x_ref.shape
    half = rows // 2
    _, n_plane, _, ch, width = r_src.shape
    nz = PLANES
    main = tokens // 128 * 128
    tail = tokens - main
    tiles = main // 128
    plane_rows = n_plane * rows
    grp = lax.axis_index("grp")
    dev = lax.axis_index("dev")
    z = dev // 2
    core = lax.rem(dev, 2)
    q = grp * 2 + core
    low = z < nz // 2
    inner = (z == 1) | (z == 2)
    outer = (z == 0) | (z == nz - 1)
    ahead = (grp, jnp.where(low, dev + 2, dev - 2))
    side = jnp.where(low, 0, nz - 1)
    own_inner = jnp.where(low, 1, 2)
    far_inner = nz - 1 - own_inner
    far_side = nz - 1 - side

    def plane_peer(other):
        return (other // 2, z * 2 + lax.rem(other, 2))

    def at_plane(other, zz):
        return (other // 2, zz * 2 + lax.rem(other, 2))

    def other_of(o):
        return lax.rem(q + o, n_plane)

    loads = [
        pltpu.make_async_copy(src, dst, in_sem.at[k])
        for k, (src, dst) in enumerate([
            (x_hbm, x_ref), (mask_hbm, mask_ref), (mask_hbm, mask_s), (wrg_hbm, wrg_ref), (wr_hbm, wr_ref),
            (wlg_hbm, wlg_ref), (wl_hbm, wl_ref), (wog_hbm, wog_ref), (wo_hbm, wo_ref)])
    ]
    for load in loads:
        load.start()

    barrier = pltpu.get_barrier_semaphore()

    @pl.loop(1, n_plane)
    def _(o):
        pl.semaphore_signal(barrier, inc=1, device_id=plane_peer(other_of(o)), device_id_type=MESH)

    @pl.when(inner)
    def _():
        pl.semaphore_signal(barrier, inc=1, device_id=ahead, device_id_type=MESH)
        pl.semaphore_signal(barrier, inc=1, device_id=at_plane(q, side), device_id_type=MESH)

    @pl.when(outer)
    def _():
        @pl.loop(0, n_plane)
        def _(k):
            pl.semaphore_signal(barrier, inc=1, device_id=at_plane(k, own_inner), device_id_type=MESH)

    for load in loads[:5]:
        load.wait()
    mask = mask_ref[...].astype(jnp.float32).reshape(1, tokens)
    pieces = [mask[:, :main], mask[:, :main]]
    if tail:
        pieces += [mask[:, main:], mask[:, main:]]
    mask2 = jnp.concatenate(pieces, axis=1)
    lane = lax.broadcasted_iota(jnp.int32, (1, width), 1)
    first = (lane < main) | ((lane >= 2 * main) & (lane < 2 * main + tail))
    row0 = (grp * n_dev + dev) * rows

    def norm_rows(v):
        v = v.astype(jnp.float32)
        c = v - jnp.mean(v, axis=-1, keepdims=True)
        var = jnp.mean(c * c, axis=-1, keepdims=True)
        return (c * lax.rsqrt(var + EPSILON)).astype(jnp.bfloat16)

    def project(n, p, wg_t, wv_t, dst):
        nt = (((1,), (1,)), ((), ()))
        gate = lax.dot_general(wg_t, n, nt, preferred_element_type=jnp.float32)
        value = lax.dot_general(wv_t, n, nt, preferred_element_type=jnp.float32)
        m0 = mask_s[row0 + p].astype(jnp.float32)
        m1 = mask_s[row0 + half + p].astype(jnp.float32)
        m = mask2 * jnp.where(first, m0, m1)
        res = (sigmoid(gate) * value * m).astype(jnp.bfloat16)
        for k in range(n_plane):
            for f in range(HALVES):
                lo = (k * HALVES + f) * ch
                dst[f, k, p] = res[lo:lo + ch]

    wrg_t, wr_t = wrg_ref[...].T, wr_ref[...].T

    @pl.loop(0, half)
    def _(p):
        a, b = norm_rows(x_ref[p]), norm_rows(x_ref[p + half])
        parts = [a[:main], b[:main]]
        if tail:
            parts += [a[main:], b[main:]]
        n = jnp.concatenate(parts, axis=0)
        nbuf[p] = n
        project(n, p, wrg_t, wr_t, r_src)

    pl.semaphore_wait(barrier, n_plane - 1 + jnp.where(inner, 1 + n_plane, 1))

    def plane_copy(src, dst, send, recv, to):
        return pltpu.make_async_remote_copy(
            src_ref=src, dst_ref=dst, send_sem=send, recv_sem=recv,
            device_id=plane_peer(to), device_id_type=MESH)

    def z_copy(src, f, zz, s):
        return pltpu.make_async_remote_copy(
            src_ref=src, dst_ref=r_buf.at[f, zz, s], send_sem=z_send.at[f, zz, s],
            recv_sem=r_recv.at[f, zz, s], device_id=ahead, device_id_type=MESH)

    def lz_copy(f, s):
        return pltpu.make_async_remote_copy(
            src_ref=l_buf.at[f, 0, s], dst_ref=l_buf.at[f, 1, s], send_sem=lz_send.at[f, s],
            recv_sem=l_recv.at[f, 1, s], device_id=ahead, device_id_type=MESH)

    def ra_copy(f, o):
        t = other_of(o)
        return plane_copy(r_src.at[f, t], r_buf.at[f, z, q], ra_send.at[f, o], r_recv.at[f, z, q], t)

    def l_copy(f, o):
        t = other_of(o)
        return plane_copy(l_src.at[f, t], l_buf.at[f, 0, q], l_send.at[f, o], l_recv.at[f, 0, q], t)

    def p_copy(f, w, t):
        return pltpu.make_async_remote_copy(
            src_ref=p_src.at[f, w, t], dst_ref=p_buf.at[f, q], send_sem=p_send.at[f, w, t],
            recv_sem=p_recv.at[f, q], device_id=at_plane(t, side if w else z), device_id_type=MESH)

    def wait_on(dst, recv):
        pltpu.make_async_remote_copy(
            src_ref=dst, dst_ref=dst, send_sem=recv, recv_sem=recv,
            device_id=ahead, device_id_type=MESH).wait_recv()

    def send_plane(f):
        @pl.loop(1, n_plane)
        def _(o):
            ra_copy(f, o).start()

    def send_left(f):
        @pl.loop(1, n_plane)
        def _(o):
            l_copy(f, o).start()

    send_plane(0)
    z_copy(r_src.at[0, q], 0, z, q).start()
    own_r = [pltpu.make_async_copy(r_src.at[f, q], r_buf.at[f, z, q], loc_sem.at[f]) for f in range(HALVES)]
    for copy in own_r:
        copy.start()

    for load in loads[5:]:
        load.wait()
    wlg_t, wl_t = wlg_ref[...].T, wl_ref[...].T

    @pl.loop(0, half)
    def _(p):
        project(nbuf[p], p, wlg_t, wl_t, l_src)

    own_l = [pltpu.make_async_copy(l_src.at[f, q], l_buf.at[f, 0, q], loc_sem.at[HALVES + f]) for f in range(HALVES)]
    for copy in own_l:
        copy.start()

    @pl.loop(1, n_plane)
    def _(o):
        s = other_of(o)
        wait_on(r_buf.at[0, z, s], r_recv.at[0, z, s])
        z_copy(r_buf.at[0, z, s], 0, z, s).start()

    send_left(0)

    wog = wog_ref[...]

    @pl.loop(0, half)
    def _(p):
        g = sigmoid(jnp.dot(nbuf[p], wog, preferred_element_type=jnp.float32)).astype(jnp.bfloat16)
        out_ref[p, :main] = g[:main]
        out_ref[p + half, :main] = g[main:2 * main]
        if tail:
            out_ref[p, main:] = g[2 * main:2 * main + tail]
            out_ref[p + half, main:] = g[2 * main + tail:]

    lane1 = lax.broadcasted_iota(jnp.int32, (1, 128), 1)

    def unpack(block, s, masked):
        for p in range(half):
            v = block[p].astype(jnp.float32)
            for b in range(2):
                where = pl.ds(s * rows + p + b * half, ch, stride=plane_rows)
                for t in range(tiles):
                    stage[t, where, :] = v[:, b * main + t * 128:b * main + (t + 1) * 128]
                if tail:
                    u = v[:, 2 * main:]
                    if b:
                        u = pltpu.roll(u, tail, 1)
                    if masked:
                        u = jnp.where(lane1 < tail, u, 0.0)
                    stage[tiles, where, :] = u

    n_tiles = tiles + (1 if tail else 0)

    def settle(dst):
        for c in range(ch):
            for t in range(n_tiles):
                dst(c, t, stage[t, c * plane_rows:(c + 1) * plane_rows, :].astype(jnp.bfloat16))

    for copy in own_r + own_l:
        copy.wait()

    def wait_left(f):
        @pl.loop(1, n_plane)
        def _(o):
            s = other_of(o)
            wait_on(l_buf.at[f, 0, s], l_recv.at[f, 0, s])

    def wait_right(f):
        @pl.loop(1, n_plane)
        def _(o):
            s = other_of(o)
            wait_on(r_buf.at[f, z, s], r_recv.at[f, z, s])

    wait_left(0)
    for f in range(1, HALVES):
        send_plane(f)

    @pl.when(outer)
    def _():
        @pl.loop(0, n_plane)
        def _(s):
            lz_copy(0, s).start()

    for f in range(1, HALVES):
        wait_right(f)
        send_left(f)

    @pl.when(outer)
    def _():
        for f in range(1, HALVES):
            @pl.loop(0, n_plane)
            def _(s):
                z_copy(r_buf.at[f - 1, z, s], f - 1, z, s).wait_send()

            @pl.loop(0, n_plane)
            def _(s):
                z_copy(r_buf.at[f, z, s], f, z, s).start()

            wait_left(f)

            @pl.loop(0, n_plane)
            def _(s):
                lz_copy(f - 1, s).wait_send()

            @pl.loop(0, n_plane)
            def _(s):
                lz_copy(f, s).start()

        @pl.loop(0, n_plane)
        def _(s):
            z_copy(r_buf.at[HALVES - 1, z, s], HALVES - 1, z, s).wait_send()
            lz_copy(HALVES - 1, s).wait_send()

    def take_left(f, w):
        @pl.loop(0, n_plane)
        def _(s):
            unpack(l_buf.at[f, w, s], s, True)

        def to_left(c, t, v):
            l_mat[c, :, t * 128:(t + 1) * 128] = v

        settle(to_left)

    def take_plane(f, zz):
        @pl.loop(0, n_plane)
        def _(s):
            unpack(r_buf.at[f, zz, s], s, False)

        def to_right(c, t, v):
            r_mat[c, zz, :, t * 128:(t + 1) * 128] = v

        settle(to_right)

    def multiply(f, w):
        for c in range(ch):
            prod = lax.dot_general(
                l_mat[c], r_mat[c].reshape(nz * plane_rows, n_tiles * 128), (((1,), (1,)), ((), ())),
                preferred_element_type=jnp.float32)
            for t in range(tiles):
                stage[t, c * plane_rows:(c + 1) * plane_rows, :] = prod[:, t * 128:(t + 1) * 128]
            if tail:
                stage[tiles, c * plane_rows:(c + 1) * plane_rows, :tail] = prod[:, main:]

        @pl.loop(1, n_plane + 1)
        def _(o):
            to = other_of(o)
            for p in range(half):
                pair = []
                ends = []
                for b in range(2):
                    where = pl.ds(to * rows + p + b * half, ch, stride=plane_rows)
                    pair += [stage[t, where, :] for t in range(tiles)]
                    if tail:
                        ends.append(stage[tiles, where, :])
                if tail:
                    pair.append(jnp.where(lane1 < tail, ends[0], pltpu.roll(ends[1], tail, 1)))
                p_src[f, w, to, p] = jnp.concatenate(pair, axis=1).astype(jnp.bfloat16)

            if w:
                p_copy(f, w, to).start()
            else:
                @pl.when(o < n_plane)
                def _():
                    p_copy(f, w, to).start()

    def local_p(f):
        return pltpu.make_async_copy(p_src.at[f, 0, q], p_buf.at[f, q], loc_sem.at[2 * HALVES + f])

    @pl.when(inner)
    def _():
        for f in range(HALVES):
            take_plane(f, z)

            @pl.loop(0, n_plane)
            def _(s):
                wait_on(r_buf.at[f, side, s], r_recv.at[f, side, s])
                z_copy(r_buf.at[f, side, s], f, side, s).start()

            take_plane(f, side)

            @pl.loop(0, n_plane)
            def _(s):
                wait_on(r_buf.at[f, far_inner, s], r_recv.at[f, far_inner, s])

            take_plane(f, far_inner)

            @pl.loop(0, n_plane)
            def _(s):
                wait_on(r_buf.at[f, far_side, s], r_recv.at[f, far_side, s])

            if f + 1 < HALVES:
                @pl.loop(0, n_plane)
                def _(s):
                    z_copy(r_buf.at[f + 1, z, s], f + 1, z, s).start()

                wait_left(f + 1)

            take_plane(f, far_side)

            @pl.loop(0, n_plane)
            def _(s):
                wait_on(l_buf.at[f, 1, s], l_recv.at[f, 1, s])

            take_left(f, 1)
            multiply(f, 1)
            take_left(f, 0)
            multiply(f, 0)
            local_p(f).start()

        for f in range(HALVES):
            local_p(f).wait()

            @pl.loop(1, n_plane)
            def _(o):
                s = other_of(o)
                wait_on(p_buf.at[f, s], p_recv.at[f, s])

    @pl.when(outer)
    def _():
        for f in range(HALVES):
            @pl.loop(0, n_plane)
            def _(s):
                wait_on(p_buf.at[f, s], p_recv.at[f, s])

    wo = wo_ref[...]
    piece = 2 * rows

    @pl.loop(0, half)
    def _(p):
        v = jnp.concatenate(
            [p_buf[f, k, p].astype(jnp.float32) for k in range(n_plane) for f in range(HALVES)], axis=0)
        c = v - jnp.mean(v, axis=0, keepdims=True)
        var = jnp.mean(c * c, axis=0, keepdims=True)
        n = (c * lax.rsqrt(var + EPSILON)).astype(jnp.bfloat16)
        y = lax.dot_general(n, wo, (((0,), (0,)), ((), ())), preferred_element_type=jnp.float32)
        for b in range(2):
            parts = [y[b * main:(b + 1) * main]]
            if tail:
                parts.append(y[2 * main + b * tail:2 * main + (b + 1) * tail])
            full = jnp.concatenate(parts, axis=0)
            for zz in range(nz):
                for gg in range(n_grp):
                    y_buf[b, (gg * nz + zz) * piece:(gg * nz + zz + 1) * piece, :] = (
                        full[(zz * n_grp + gg) * piece:(zz * n_grp + gg + 1) * piece])
            row = p + b * half
            out_ref[row] = (y_buf[b] * out_ref[row].astype(jnp.float32)).astype(jnp.bfloat16)

    for f in range(HALVES):
        @pl.loop(1, n_plane)
        def _(o):
            ra_copy(f, o).wait_send()
            l_copy(f, o).wait_send()

        @pl.when(inner)
        def _():
            @pl.loop(1, n_plane)
            def _(o):
                p_copy(f, 0, other_of(o)).wait_send()

            @pl.loop(0, n_plane)
            def _(s):
                p_copy(f, 1, s).wait_send()
                z_copy(r_buf.at[f, z, s], f, z, s).wait_send()
                z_copy(r_buf.at[f, side, s], f, side, s).wait_send()


def fused(mesh, args):
    n_grp, n_dev = mesh.shape["grp"], mesh.shape["dev"]
    x = args[0]
    rows, tokens, chans = x.shape
    n_plane, nz, half = n_grp * 2, n_dev // 2, rows // 2
    ch = args[1].shape[1] // n_plane // HALVES
    width = 2 * tokens
    n_tiles = -(-tokens // 128)
    bf, f32 = jnp.bfloat16, jnp.float32
    blocks = (n_plane, half, ch, width)
    whole = (HALVES,) + blocks
    weight = pltpu.VMEM(args[1].shape, bf)
    hbm = pl.BlockSpec(memory_space=pltpu.HBM)
    vmem = pl.BlockSpec(memory_space=pltpu.VMEM)
    dma = pltpu.SemaphoreType.DMA
    return pl.pallas_call(
        functools.partial(fused_kernel, n_grp, n_dev),
        out_shape=jax.ShapeDtypeStruct(x.shape, bf),
        in_specs=[hbm] * 8,
        out_specs=vmem,
        scratch_shapes=[
            pltpu.VMEM(x.shape, bf),
            weight, weight, weight, weight, weight, weight,
            pltpu.VMEM((tokens,), jnp.int32),
            pltpu.SMEM((tokens,), jnp.int32),
            pltpu.VMEM((half, width, chans), bf),
            pltpu.VMEM(whole, bf),
            pltpu.VMEM(whole, bf),
            pltpu.VMEM((HALVES, 2) + blocks, bf),
            pltpu.VMEM((HALVES, nz) + blocks, bf),
            pltpu.VMEM((HALVES, 2) + blocks, bf),
            pltpu.VMEM(whole, bf),
            pltpu.VMEM((n_tiles, ch * n_plane * rows, 128), f32),
            pltpu.VMEM((ch, n_plane * rows, n_tiles * 128), bf),
            pltpu.VMEM((ch, nz, n_plane * rows, n_tiles * 128), bf),
            pltpu.VMEM((2, tokens, chans), f32),
            dma((HALVES, n_plane)),
            dma((HALVES, n_plane)),
            dma((HALVES, 2, n_plane)),
            dma((HALVES, nz, n_plane)),
            dma((HALVES, n_plane)),
            dma((HALVES, nz, n_plane)),
            dma((HALVES, 2, n_plane)),
            dma((HALVES, n_plane)),
            dma((3 * HALVES,)),
            dma((9,)),
        ],
        compiler_params=pltpu.CompilerParams(
            collective_id=0, has_side_effects=True, vmem_limit_bytes=56 * 1024 * 1024),
        cost_estimate=pl.CostEstimate(flops=10**9, bytes_accessed=10**7, transcendentals=10**6),
    )(*args)


def fits(mesh, tokens, hidden):
    n_plane, nz = mesh.shape["grp"] * 2, mesh.shape["dev"] // 2
    rows = tokens // (n_plane * nz)
    if mesh.shape["dev"] != 2 * PLANES or hidden % n_plane or (hidden // n_plane) % 16:
        return False
    if rows % 2 or (n_plane * rows) % 16 or tokens % 128 not in (0, 64):
        return False
    return 4 * (hidden // n_plane) * tokens * tokens < 16 * 1024 * 1024


def solution(mesh):
    def body(*args):
        if fits(mesh, args[-1].shape[0], args[1].shape[1]):
            return fused(mesh, args)
        return local(*args)

    return jax.shard_map(
        body,
        mesh=mesh,
        in_specs=(P(("grp", "dev"), None, None), P(), P(), P(), P(), P(), P(), P()),
        out_specs=P(("grp", "dev"), None, None),
        check_vma=False,
    )
```

time: 89.6 us -> 76.2 us (0.85)
  Pallas kernels: 81.2 us -> 73.9 us
  local copies, waits for them, and re-layouts: 7.34 us -> 2.1 us
    pallas_call x1, Pallas kernels: 81.2 us -> 73.9 us  [fused(): pl.pallas_call(functools.partial(fused_kernel, n_grp, n_dev), out_shape=j...]
    unnamed x17 -> x1, local copies, waits for them, and re-layouts: 6.59 us -> 2.1 us
where the time goes in v2:
time: 76.2 us; the launch traced here: 76 us
  Pallas kernels  73.9 us (97%)
  local copies, waits for them, and re-layouts  2.1 us (3%)
    pallas_call x1, Pallas kernels, fused(): pl.pallas_call(functools.partial(fused_kernel, n_grp, n_dev), out_shape=j...  73.9 us
    unnamed x1, local copies, waits for them, and re-layouts  2.1 us

profile of v2, /device:TPU:0, one launch (start us, length us, event | category | flops | bytes accessed | tf_op | source)
XLA Modules:
  0.0 76.0 jit_solution(7892991840800198856)
XLA Ops:
  0.0 73.9 %shard_map.82 = bf16[10,320,128]{2,1,0:T(8,128)(2,1)} custom-call(bf16[10,320,128]{2,1,0:T(8,128)(2,1)} %x_hbm.1, bf16[128,128]{1,0:T(8,128)(2,1)} %wlg_hbm.1, bf16[128,128]{1,0:T(8,128)(2,1)} %wl_hbm.1, bf16[128,128]{1,0:T(8,128)(2,1)} %wrg_hbm.1, bf16[128,128]{1,0:T(8,128)(2,1)} %wr_hbm.1, bf16[128,128]{1,0:T(8,128)(2,1)} %wog_hbm.1, ...), custom_call_target="tpu_custom_call" | custom-call | flops 1000000000 | bytes 10000000 | tf_op jit(solution)/shard_map/pallas_call | solution.py:500
  73.9 2.1 %copy.10 = bf16[10,320,128]{2,1,0:T(8,128)(2,1)} copy(bf16[10,320,128]{2,1,0:T(8,128)(2,1)} %shard_map.82) | data formatting | bytes 1638400

commit v3 on v2

--- a/solution.py
+++ b/solution.py
@@ -231,13 +231,17 @@
     for copy in own_l:
         copy.start()
 
+    send_left(0)
+
     @pl.loop(1, n_plane)
     def _(o):
         s = other_of(o)
         wait_on(r_buf.at[0, z, s], r_recv.at[0, z, s])
         z_copy(r_buf.at[0, z, s], 0, z, s).start()
 
-    send_left(0)
+    for f in range(1, HALVES):
+        send_plane(f)
+        send_left(f)
 
     wog = wog_ref[...]
 
@@ -290,9 +294,6 @@
             wait_on(r_buf.at[f, z, s], r_recv.at[f, z, s])
 
     wait_left(0)
-    for f in range(1, HALVES):
-        send_plane(f)
-
     @pl.when(outer)
     def _():
         @pl.loop(0, n_plane)
@@ -301,33 +302,25 @@
 
     for f in range(1, HALVES):
         wait_right(f)
-        send_left(f)
 
     @pl.when(outer)
     def _():
         for f in range(1, HALVES):
             @pl.loop(0, n_plane)
             def _(s):
-                z_copy(r_buf.at[f - 1, z, s], f - 1, z, s).wait_send()
-
-            @pl.loop(0, n_plane)
-            def _(s):
                 z_copy(r_buf.at[f, z, s], f, z, s).start()
 
             wait_left(f)
 
             @pl.loop(0, n_plane)
             def _(s):
-                lz_copy(f - 1, s).wait_send()
-
-            @pl.loop(0, n_plane)
-            def _(s):
                 lz_copy(f, s).start()
 
-        @pl.loop(0, n_plane)
-        def _(s):
-            z_copy(r_buf.at[HALVES - 1, z, s], HALVES - 1, z, s).wait_send()
-            lz_copy(HALVES - 1, s).wait_send()
+        for f in range(HALVES):
+            @pl.loop(0, n_plane)
+            def _(s):
+                z_copy(r_buf.at[f, z, s], f, z, s).wait_send()
+                lz_copy(f, s).wait_send()
 
     def take_left(f, w):
         @pl.loop(0, n_plane)

time: 76.2 us -> 72.1 us (0.946)
  Pallas kernels: 73.9 us -> 69.8 us
    pallas_call x1, Pallas kernels: 73.9 us -> 69.8 us  [fused(): pl.pallas_call(functools.partial(fused_kernel, n_grp, n_dev), out_shape=j...]
where the time goes in v3:
time: 72.1 us; the launch traced here: 71.9 us
  Pallas kernels  69.8 us (97%)
  local copies, waits for them, and re-layouts  2.1 us (3%)
    pallas_call x1, Pallas kernels, fused(): pl.pallas_call(functools.partial(fused_kernel, n_grp, n_dev), out_shape=j...  69.8 us
    unnamed x1, local copies, waits for them, and re-layouts  2.1 us

profile of v3, /device:TPU:0, one launch (start us, length us, event | category | flops | bytes accessed | tf_op | source)
XLA Modules:
  0.0 71.9 jit_solution(282861697005859424)
XLA Ops:
  0.0 69.8 %shard_map.82 = bf16[10,320,128]{2,1,0:T(8,128)(2,1)} custom-call(bf16[10,320,128]{2,1,0:T(8,128)(2,1)} %x_hbm.1, bf16[128,128]{1,0:T(8,128)(2,1)} %wlg_hbm.1, bf16[128,128]{1,0:T(8,128)(2,1)} %wl_hbm.1, bf16[128,128]{1,0:T(8,128)(2,1)} %wrg_hbm.1, bf16[128,128]{1,0:T(8,128)(2,1)} %wr_hbm.1, bf16[128,128]{1,0:T(8,128)(2,1)} %wog_hbm.1, ...), custom_call_target="tpu_custom_call" | custom-call | flops 1000000000 | bytes 10000000 | tf_op jit(solution)/shard_map/pallas_call | solution.py:493
  69.8 2.1 %copy.10 = bf16[10,320,128]{2,1,0:T(8,128)(2,1)} copy(bf16[10,320,128]{2,1,0:T(8,128)(2,1)} %shard_map.82) | data formatting | bytes 1638400
